TPU v7x, 256 devices: a whole 4x4x8 slice. The times are simulated.
256 devices in a mesh: head: 16 (over y, x), blk: 16 (over z, core).
Axes of the slice: x: 4, y: 4, z: 8, core: 2. Of those that a mesh axis runs over, the one named last changes fastest.
Arguments:
- queries: bfloat16 [16, 2048, 4096], P('blk', 'head'), may hold values from -120 to 120
- keys: bfloat16 [16, 2048, 1024], P('blk', 'head'), may hold values from -5 to 5
- values: bfloat16 [16, 2048, 1024], P('blk', 'head'), may hold values from -6 to 6
- blocks: int32 [32, 16, 16, 48], P('head', 'blk'), may hold values from -1 to 15, as said below
Outputs:
- attended: bfloat16 [16, 2048, 4096], P('blk', 'head')
Inputs may be any that keep to these rules, and one draw needn't show every extreme that they name: `blocks`: entry [i, c', b, c * 3 + j] names a key block of span c (0 to 15) or is -1; the 3 slots of one span never name the same block twice unless -1.
All inputs are finite; a program needn't handle non-finite values.
Results may differ from a plain program's by a relative error of at most 0.0038.
Values may be sent and summed in bfloat16 or wider, within the bound.
A program may use at most 64 MiB of HBM per device.

v0:
```python
import jax
import jax.numpy as jnp
from jax import lax
from jax.sharding import PartitionSpec as P

HEAD_DIM = 128
BLOCK = 128
SLOTS = 3


NEG = -1e30


def shifted(value, axis, by):
    length = lax.axis_size(axis)
    pairs = [(i, i + by) for i in range(length) if 0 <= i + by < length]
    return lax.ppermute(value, axis, pairs)


def tile_terms(scores, allowed, value_tiles):
    masked = jnp.where(allowed, scores, NEG)
    row_max = jnp.max(masked, axis=-1)
    some = jnp.any(allowed, axis=-1)
    probs = jnp.where(allowed, jnp.exp(masked - row_max[..., None]), 0.0)
    row_sum = jnp.sum(probs, axis=-1)
    rounded = probs.astype(jnp.bfloat16)
    out = jnp.einsum("...qk,...kd->...qd", rounded, value_tiles, preferred_element_type=jnp.float32)
    return (jnp.where(some, row_max, NEG), row_sum, out)


def absorb(state, tile_max, tile_sum, tile_out):
    top, total, mixed = state
    new_top = jnp.maximum(top, jnp.max(tile_max, axis=-2))
    keep = jnp.exp(top - new_top)
    scale_t = jnp.exp(tile_max - new_top[..., None, :])
    total = total * keep + jnp.sum(tile_sum * scale_t, axis=-2)
    mixed = mixed * keep[..., None] + jnp.sum(tile_out * scale_t[..., None], axis=-3)
    return (new_top, total, mixed)


def body(queries, keys, values, blocks):
    n_head = lax.axis_size("head")
    n_blk = lax.axis_size("blk")
    blk_idx = lax.axis_index("blk")
    kv_heads = keys.shape[2] // HEAD_DIM
    share = max(1, n_head // kv_heads)
    tok_rows = queries.shape[1]
    wide_k = jnp.repeat(keys.reshape(1, tok_rows, kv_heads, HEAD_DIM), share, axis=2).reshape(
        1, tok_rows, -1
    )
    wide_v = jnp.repeat(values.reshape(1, tok_rows, kv_heads, HEAD_DIM), share, axis=2).reshape(
        1, tok_rows, -1
    )
    q_local, k_local, v_local = (
        lax.all_to_all(queries, "head", split_axis=2, concat_axis=1, tiled=True),
        lax.all_to_all(wide_k, "head", split_axis=2, concat_axis=1, tiled=True),
        lax.all_to_all(wide_v, "head", split_axis=2, concat_axis=1, tiled=True),
    )
    span_len = q_local.shape[1]
    nbc = span_len // BLOCK
    q_per = q_local.shape[2] // HEAD_DIM
    kv_per = k_local.shape[2] // HEAD_DIM
    group = q_per // kv_per
    scale = HEAD_DIM ** (-0.5)
    q_tiles = q_local.reshape(nbc, BLOCK, q_per, HEAD_DIM).transpose(2, 0, 1, 3)
    k_flat = (
        k_local.reshape(nbc, BLOCK, kv_per, HEAD_DIM)
        .transpose(2, 0, 1, 3)
        .reshape(kv_per * nbc, BLOCK, HEAD_DIM)
    )
    v_flat = (
        v_local.reshape(nbc, BLOCK, kv_per, HEAD_DIM)
        .transpose(2, 0, 1, 3)
        .reshape(kv_per * nbc, BLOCK, HEAD_DIM)
    )
    head_of = jnp.arange(q_per, dtype=jnp.int32) // group
    local_lists = blocks[:, 0]
    rows = blk_idx * nbc + jnp.arange(nbc, dtype=jnp.int32)
    diag_index = head_of[:, None] * nbc + jnp.arange(nbc, dtype=jnp.int32)[None, :]
    diag_k = jnp.take(k_flat, diag_index, axis=0)
    diag_v = jnp.take(v_flat, diag_index, axis=0)
    scores = (
        jnp.einsum("hrqd,hrkd->hrqk", q_tiles, diag_k, preferred_element_type=jnp.float32) * scale
    )
    causal = jnp.tril(jnp.ones((BLOCK, BLOCK), dtype=bool))
    state = tile_terms(scores, causal, diag_v)

    def span_terms(state, key_tiles, val_tiles, span_id):
        cols = lax.dynamic_slice_in_dim(local_lists, span_id * SLOTS, SLOTS, 2)
        allowed = (cols >= 0) & (span_id * nbc + cols < rows[None, :, None])
        index = head_of[:, None, None] * nbc + jnp.clip(cols, 0, nbc - 1)
        picked_k = jnp.take(key_tiles, index, axis=0)
        picked_v = jnp.take(val_tiles, index, axis=0)
        scores = (
            jnp.einsum("hrqd,hrskd->hrsqk", q_tiles, picked_k, preferred_element_type=jnp.float32)
            * scale
        )
        t_max, t_sum, t_out = tile_terms(scores, allowed[..., None, None], picked_v)
        return absorb(state, t_max, t_sum, t_out)

    state = span_terms(state, k_flat, v_flat, blk_idx)

    def cycle_step(step, carry):
        key_tiles, val_tiles, running = carry
        key_tiles, val_tiles = shifted((key_tiles, val_tiles), "blk", 1)
        span_id = (blk_idx - step) % n_blk
        return (key_tiles, val_tiles, span_terms(running, key_tiles, val_tiles, span_id))

    final = lax.fori_loop(1, n_blk, cycle_step, (k_flat, v_flat, state))[2]
    top, total, mixed = final
    result = (mixed / total[..., None]).astype(jnp.bfloat16)
    result = result.transpose(1, 2, 0, 3).reshape(1, span_len, q_per * HEAD_DIM)
    return lax.all_to_all(result, "head", split_axis=1, concat_axis=2, tiled=True)


def solution(mesh):
    placed = (
        P("blk", "head", None),
        P("blk", "head", None),
        P("blk", "head", None),
        P("head", "blk", None, None),
    )
    return jax.shard_map(
        body, mesh=mesh, in_specs=placed, out_specs=P("blk", "head", None), check_vma=False
    )
```

profile of v0, /device:TPU:97, one launch (start us, length us, event | category | flops | bytes accessed | tf_op | source)
XLA Modules:
  0.0 668.9 jit_solution(12653143317918561667)
XLA Ops:
  1.3 8.1 %copy.190 = bf16[1,128,2048]{1,0,2:T(2,128)(2,1)S(1)} copy(bf16[1,128,2048]{1,2,0:T(8,128)(2,1)S(1)} %bitcast.149) | data formatting | bytes 1048576 | tf_op jit(solution)/shard_map/broadcast_in_dim | solution.py:48
  10.0 11.6 %reduce = bf16[2048,128]{1,0:T(8,128)(2,1)S(1)} reduce(bf16[2048,1,128]{2,1,0:T(2,128)(2,1)S(1)} %bitcast.144, bf16[]{:T(256)} %broadcast.295), dimensions={1}, to_apply=%bitcast.113.reduce_sub_computation | reduce | bytes 1048578
  22.5 7.2 %all-to-all-start = ((bf16[16,2,8192]{2,1,0:T(2,128)(2,1)}), bf16[16,2,8192]{2,1,0:T(2,128)(2,1)S(1)}, u32[]{:S(2)}, u32[]{:S(2)}) async-start(bf16[16,2,8192]{2,1,0:T(2,128)(2,1)} %reshape.236), calls=%async_computation | async-start | bytes 1048576 | tf_op jit(solution)/shard_map/all_to_all | solution.py:56
  30.2 8.1 %copy.189 = bf16[1,128,2048]{1,0,2:T(2,128)(2,1)S(1)} copy(bf16[1,128,2048]{1,2,0:T(8,128)(2,1)S(1)} %bitcast.150) | data formatting | bytes 1048576 | tf_op jit(solution)/shard_map/broadcast_in_dim | solution.py:51
  38.3 11.6 %reduce.1 = bf16[2048,128]{1,0:T(8,128)(2,1)S(1)} reduce(bf16[2048,1,128]{2,1,0:T(2,128)(2,1)S(1)} %bitcast.145, bf16[]{:T(256)} %broadcast.295), dimensions={1}, to_apply=%bitcast.112.reduce_sub_computation | reduce | bytes 1048578
  50.8 7.0 %all-to-all-start.1 = ((bf16[16,2,8192]{2,1,0:T(2,128)(2,1)}), bf16[16,2,8192]{2,1,0:T(2,128)(2,1)}, u32[]{:S(2)}, u32[]{:S(2)}) async-start(bf16[16,2,8192]{2,1,0:T(2,128)(2,1)} %reshape.238), calls=%async_computation.1 | async-start | bytes 1048576 | tf_op jit(solution)/shard_map/all_to_all | solution.py:57
  60.8 22.4 %reduce.2 = bf16[4096,128]{1,0:T(8,128)(2,1)S(1)} reduce(bf16[4096,1,128]{2,1,0:T(2,128)(2,1)S(1)} %bitcast.139, bf16[]{:T(256)} %broadcast.295), dimensions={1}, to_apply=%bitcast.99.reduce_sub_computation | reduce | bytes 2097154
  84.4 7.0 %all-to-all-start.2 = ((bf16[16,2,16384]{2,1,0:T(2,128)(2,1)}), bf16[16,2,16384]{2,1,0:T(2,128)(2,1)}, u32[]{:S(2)}, u32[]{:S(2)}) async-start(bf16[16,2,16384]{2,1,0:T(2,128)(2,1)} %reshape.240), calls=%async_computation.2 | async-start | bytes 2097152 | tf_op jit(solution)/shard_map/all_to_all | solution.py:55
  136.7 493.9 %while.24 = (s32[]{:T(128)}, bf16[16,128,128]{2,1,0:T(8,128)(2,1)}, bf16[16,128,128]{2,1,0:T(8,128)(2,1)}, f32[2,16,128]{2,1,0:T(8,128)S(1)}, f32[2,16,128]{2,1,...) while((s32[]{:T(128)}, bf16[16,128,128]{2,1,0:T(8,128)(2,1)}, ...), condition=%wide.region_14.17_spmd.clone, body=%wide.region_8.16_spmd.clone.sunk | while | flops 832628928 | bytes 79339568 | solution.py:109
  136.9 6.7 %collective-permute-start = (bf16[16,128,128]{2,1,0:T(8,128)(2,1)}, bf16[16,128,128]{2,1,0:T(8,128)(2,1)S(1)}, u32[]{:S(2)}, u32[]{:S(2)}) collective-permute-start(bf16[16,128,128]{2,1,0:T(8,128)(2,1)} %get-tuple-element.484), channel_id=1, source_target_pairs={{0,1},{1,2},{2,3},{3,4},{4,5},{5,6},{6,7},{7,8},{8,9},{9,10},{10,1... | collective-permute-start | bytes 1572872 | tf_op jit(solution)/shard_map/while/body/eval_jaxpr/ppermute | solution.py:17
  161.9 6.6 multiply_reduce_fusion.7
  194.8 6.6 multiply_reduce_fusion.7
  227.6 6.6 multiply_reduce_fusion.7
  260.4 6.6 multiply_reduce_fusion.7
  293.2 6.6 multiply_reduce_fusion.7
  326.0 6.6 multiply_reduce_fusion.7
  358.9 6.6 multiply_reduce_fusion.7
  391.7 6.6 multiply_reduce_fusion.7
  424.5 6.6 multiply_reduce_fusion.7
  457.3 6.6 multiply_reduce_fusion.7
  490.2 6.6 multiply_reduce_fusion.7
  621.5 6.6 multiply_reduce_fusion.7
  632.8 10.6 %reduce.3 = bf16[2048,256]{1,0:T(8,128)(2,1)S(1)} reduce(bf16[2048,1,256]{2,1,0:T(2,128)(2,1)S(1)} %bitcast.138, bf16[]{:T(256)} %broadcast.295), dimensions={1}, to_apply=%bitcast.101.reduce_sub_computation | reduce | bytes 2097154
  643.8 21.4 %all_to_all.63 = bf16[16,2,16384]{2,1,0:T(2,128)(2,1)S(1)} all-to-all(bf16[16,2,16384]{2,1,0:T(2,128)(2,1)S(1)} %reshape.242), channel_id=1, replica_groups=mesh['head'=16,'blk'=16] {'head'}, dimensions={0} | all-to-all | bytes 2097152 | tf_op jit(solution)/shard_map/all_to_all | solution.py:113
  (432 shorter events, 463.7 us)
Async XLA Ops:
  22.5 28.4 %all-to-all-start = ((bf16[16,2,8192]{2,1,0:T(2,128)(2,1)}), bf16[16,2,8192]{2,1,0:T(2,128)(2,1)S(1)}, u32[]{:S(2)}, u32[]{:S(2)}) async-start(bf16[16,2,8192]{2,1,0:T(2,128)(2,1)} %reshape.236), calls=%async_computation | async-start | bytes 1048576 | tf_op jit(solution)/shard_map/all_to_all | solution.py:56
  50.8 33.5 %all-to-all-start.1 = ((bf16[16,2,8192]{2,1,0:T(2,128)(2,1)}), bf16[16,2,8192]{2,1,0:T(2,128)(2,1)}, u32[]{:S(2)}, u32[]{:S(2)}) async-start(bf16[16,2,8192]{2,1,0:T(2,128)(2,1)} %reshape.238), calls=%async_computation.1 | async-start | bytes 1048576 | tf_op jit(solution)/shard_map/all_to_all | solution.py:57
  84.4 33.8 %all-to-all-start.2 = ((bf16[16,2,16384]{2,1,0:T(2,128)(2,1)}), bf16[16,2,16384]{2,1,0:T(2,128)(2,1)}, u32[]{:S(2)}, u32[]{:S(2)}) async-start(bf16[16,2,16384]{2,1,0:T(2,128)(2,1)} %reshape.240), calls=%async_computation.2 | async-start | bytes 2097152 | tf_op jit(solution)/shard_map/all_to_all | solution.py:55
  136.9 13.2 %collective-permute-start = (bf16[16,128,128]{2,1,0:T(8,128)(2,1)}, bf16[16,128,128]{2,1,0:T(8,128)(2,1)S(1)}, u32[]{:S(2)}, u32[]{:S(2)}) collective-permute-start(bf16[16,128,128]{2,1,0:T(8,128)(2,1)} %get-tuple-element.484), channel_id=1, source_target_pairs={{0,1},{1,2},{2,3},{3,4},{4,5},{5,6},{6,7},{7,8},{8,9},{9,10},{10,1... | collective-permute-start | bytes 1572872 | tf_op jit(solution)/shard_map/while/body/eval_jaxpr/ppermute | solution.py:17
  143.7 15.5 %collective-permute-start.1 = (bf16[16,128,128]{2,1,0:T(8,128)(2,1)}, bf16[16,128,128]{2,1,0:T(8,128)(2,1)S(1)}, u32[]{:S(2)}, u32[]{:S(2)}) collective-permute-start(bf16[16,128,128]{2,1,0:T(8,128)(2,1)} %get-tuple-element.485), channel_id=1, source_target_pairs={{0,1},{1,2},{2,3},{3,4},{4,5},{5,6},{6,7},{7,8},{8,9},{9,10},{10,1... | collective-permute-start | bytes 1572872 | tf_op jit(solution)/shard_map/while/body/eval_jaxpr/ppermute | solution.py:17
  176.5 15.5 %collective-permute-start.1 = (bf16[16,128,128]{2,1,0:T(8,128)(2,1)}, bf16[16,128,128]{2,1,0:T(8,128)(2,1)S(1)}, u32[]{:S(2)}, u32[]{:S(2)}) collective-permute-start(bf16[16,128,128]{2,1,0:T(8,128)(2,1)} %get-tuple-element.485), channel_id=1, source_target_pairs={{0,1},{1,2},{2,3},{3,4},{4,5},{5,6},{6,7},{7,8},{8,9},{9,10},{10,1... | collective-permute-start | bytes 1572872 | tf_op jit(solution)/shard_map/while/body/eval_jaxpr/ppermute | solution.py:17
  209.3 15.5 %collective-permute-start.1 = (bf16[16,128,128]{2,1,0:T(8,128)(2,1)}, bf16[16,128,128]{2,1,0:T(8,128)(2,1)S(1)}, u32[]{:S(2)}, u32[]{:S(2)}) collective-permute-start(bf16[16,128,128]{2,1,0:T(8,128)(2,1)} %get-tuple-element.485), channel_id=1, source_target_pairs={{0,1},{1,2},{2,3},{3,4},{4,5},{5,6},{6,7},{7,8},{8,9},{9,10},{10,1... | collective-permute-start | bytes 1572872 | tf_op jit(solution)/shard_map/while/body/eval_jaxpr/ppermute | solution.py:17
  236.6 11.9 %collective-permute-start = (bf16[16,128,128]{2,1,0:T(8,128)(2,1)}, bf16[16,128,128]{2,1,0:T(8,128)(2,1)S(1)}, u32[]{:S(2)}, u32[]{:S(2)}) collective-permute-start(bf16[16,128,128]{2,1,0:T(8,128)(2,1)} %get-tuple-element.484), channel_id=1, source_target_pairs={{0,1},{1,2},{2,3},{3,4},{4,5},{5,6},{6,7},{7,8},{8,9},{9,10},{10,1... | collective-permute-start | bytes 1572872 | tf_op jit(solution)/shard_map/while/body/eval_jaxpr/ppermute | solution.py:17
  242.1 15.5 %collective-permute-start.1 = (bf16[16,128,128]{2,1,0:T(8,128)(2,1)}, bf16[16,128,128]{2,1,0:T(8,128)(2,1)S(1)}, u32[]{:S(2)}, u32[]{:S(2)}) collective-permute-start(bf16[16,128,128]{2,1,0:T(8,128)(2,1)} %get-tuple-element.485), channel_id=1, source_target_pairs={{0,1},{1,2},{2,3},{3,4},{4,5},{5,6},{6,7},{7,8},{8,9},{9,10},{10,1... | collective-permute-start | bytes 1572872 | tf_op jit(solution)/shard_map/while/body/eval_jaxpr/ppermute | solution.py:17
  269.5 11.9 %collective-permute-start = (bf16[16,128,128]{2,1,0:T(8,128)(2,1)}, bf16[16,128,128]{2,1,0:T(8,128)(2,1)S(1)}, u32[]{:S(2)}, u32[]{:S(2)}) collective-permute-start(bf16[16,128,128]{2,1,0:T(8,128)(2,1)} %get-tuple-element.484), channel_id=1, source_target_pairs={{0,1},{1,2},{2,3},{3,4},{4,5},{5,6},{6,7},{7,8},{8,9},{9,10},{10,1... | collective-permute-start | bytes 1572872 | tf_op jit(solution)/shard_map/while/body/eval_jaxpr/ppermute | solution.py:17
  275.0 15.5 %collective-permute-start.1 = (bf16[16,128,128]{2,1,0:T(8,128)(2,1)}, bf16[16,128,128]{2,1,0:T(8,128)(2,1)S(1)}, u32[]{:S(2)}, u32[]{:S(2)}) collective-permute-start(bf16[16,128,128]{2,1,0:T(8,128)(2,1)} %get-tuple-element.485), channel_id=1, source_target_pairs={{0,1},{1,2},{2,3},{3,4},{4,5},{5,6},{6,7},{7,8},{8,9},{9,10},{10,1... | collective-permute-start | bytes 1572872 | tf_op jit(solution)/shard_map/while/body/eval_jaxpr/ppermute | solution.py:17
  302.3 11.9 %collective-permute-start = (bf16[16,128,128]{2,1,0:T(8,128)(2,1)}, bf16[16,128,128]{2,1,0:T(8,128)(2,1)S(1)}, u32[]{:S(2)}, u32[]{:S(2)}) collective-permute-start(bf16[16,128,128]{2,1,0:T(8,128)(2,1)} %get-tuple-element.484), channel_id=1, source_target_pairs={{0,1},{1,2},{2,3},{3,4},{4,5},{5,6},{6,7},{7,8},{8,9},{9,10},{10,1... | collective-permute-start | bytes 1572872 | tf_op jit(solution)/shard_map/while/body/eval_jaxpr/ppermute | solution.py:17
  307.8 15.5 %collective-permute-start.1 = (bf16[16,128,128]{2,1,0:T(8,128)(2,1)}, bf16[16,128,128]{2,1,0:T(8,128)(2,1)S(1)}, u32[]{:S(2)}, u32[]{:S(2)}) collective-permute-start(bf16[16,128,128]{2,1,0:T(8,128)(2,1)} %get-tuple-element.485), channel_id=1, source_target_pairs={{0,1},{1,2},{2,3},{3,4},{4,5},{5,6},{6,7},{7,8},{8,9},{9,10},{10,1... | collective-permute-start | bytes 1572872 | tf_op jit(solution)/shard_map/while/body/eval_jaxpr/ppermute | solution.py:17
  340.6 15.5 %collective-permute-start.1 = (bf16[16,128,128]{2,1,0:T(8,128)(2,1)}, bf16[16,128,128]{2,1,0:T(8,128)(2,1)S(1)}, u32[]{:S(2)}, u32[]{:S(2)}) collective-permute-start(bf16[16,128,128]{2,1,0:T(8,128)(2,1)} %get-tuple-element.485), channel_id=1, source_target_pairs={{0,1},{1,2},{2,3},{3,4},{4,5},{5,6},{6,7},{7,8},{8,9},{9,10},{10,1... | collective-permute-start | bytes 1572872 | tf_op jit(solution)/shard_map/while/body/eval_jaxpr/ppermute | solution.py:17
  373.4 15.5 %collective-permute-start.1 = (bf16[16,128,128]{2,1,0:T(8,128)(2,1)}, bf16[16,128,128]{2,1,0:T(8,128)(2,1)S(1)}, u32[]{:S(2)}, u32[]{:S(2)}) collective-permute-start(bf16[16,128,128]{2,1,0:T(8,128)(2,1)} %get-tuple-element.485), channel_id=1, source_target_pairs={{0,1},{1,2},{2,3},{3,4},{4,5},{5,6},{6,7},{7,8},{8,9},{9,10},{10,1... | collective-permute-start | bytes 1572872 | tf_op jit(solution)/shard_map/while/body/eval_jaxpr/ppermute | solution.py:17
  400.8 11.9 %collective-permute-start = (bf16[16,128,128]{2,1,0:T(8,128)(2,1)}, bf16[16,128,128]{2,1,0:T(8,128)(2,1)S(1)}, u32[]{:S(2)}, u32[]{:S(2)}) collective-permute-start(bf16[16,128,128]{2,1,0:T(8,128)(2,1)} %get-tuple-element.484), channel_id=1, source_target_pairs={{0,1},{1,2},{2,3},{3,4},{4,5},{5,6},{6,7},{7,8},{8,9},{9,10},{10,1... | collective-permute-start | bytes 1572872 | tf_op jit(solution)/shard_map/while/body/eval_jaxpr/ppermute | solution.py:17
  406.3 15.5 %collective-permute-start.1 = (bf16[16,128,128]{2,1,0:T(8,128)(2,1)}, bf16[16,128,128]{2,1,0:T(8,128)(2,1)S(1)}, u32[]{:S(2)}, u32[]{:S(2)}) collective-permute-start(bf16[16,128,128]{2,1,0:T(8,128)(2,1)} %get-tuple-element.485), channel_id=1, source_target_pairs={{0,1},{1,2},{2,3},{3,4},{4,5},{5,6},{6,7},{7,8},{8,9},{9,10},{10,1... | collective-permute-start | bytes 1572872 | tf_op jit(solution)/shard_map/while/body/eval_jaxpr/ppermute | solution.py:17
  433.6 11.9 %collective-permute-start = (bf16[16,128,128]{2,1,0:T(8,128)(2,1)}, bf16[16,128,128]{2,1,0:T(8,128)(2,1)S(1)}, u32[]{:S(2)}, u32[]{:S(2)}) collective-permute-start(bf16[16,128,128]{2,1,0:T(8,128)(2,1)} %get-tuple-element.484), channel_id=1, source_target_pairs={{0,1},{1,2},{2,3},{3,4},{4,5},{5,6},{6,7},{7,8},{8,9},{9,10},{10,1... | collective-permute-start | bytes 1572872 | tf_op jit(solution)/shard_map/while/body/eval_jaxpr/ppermute | solution.py:17
  439.1 15.5 %collective-permute-start.1 = (bf16[16,128,128]{2,1,0:T(8,128)(2,1)}, bf16[16,128,128]{2,1,0:T(8,128)(2,1)S(1)}, u32[]{:S(2)}, u32[]{:S(2)}) collective-permute-start(bf16[16,128,128]{2,1,0:T(8,128)(2,1)} %get-tuple-element.485), channel_id=1, source_target_pairs={{0,1},{1,2},{2,3},{3,4},{4,5},{5,6},{6,7},{7,8},{8,9},{9,10},{10,1... | collective-permute-start | bytes 1572872 | tf_op jit(solution)/shard_map/while/body/eval_jaxpr/ppermute | solution.py:17
  471.9 15.5 %collective-permute-start.1 = (bf16[16,128,128]{2,1,0:T(8,128)(2,1)}, bf16[16,128,128]{2,1,0:T(8,128)(2,1)S(1)}, u32[]{:S(2)}, u32[]{:S(2)}) collective-permute-start(bf16[16,128,128]{2,1,0:T(8,128)(2,1)} %get-tuple-element.485), channel_id=1, source_target_pairs={{0,1},{1,2},{2,3},{3,4},{4,5},{5,6},{6,7},{7,8},{8,9},{9,10},{10,1... | collective-permute-start | bytes 1572872 | tf_op jit(solution)/shard_map/while/body/eval_jaxpr/ppermute | solution.py:17
  504.7 15.5 %collective-permute-start.1 = (bf16[16,128,128]{2,1,0:T(8,128)(2,1)}, bf16[16,128,128]{2,1,0:T(8,128)(2,1)S(1)}, u32[]{:S(2)}, u32[]{:S(2)}) collective-permute-start(bf16[16,128,128]{2,1,0:T(8,128)(2,1)} %get-tuple-element.485), channel_id=1, source_target_pairs={{0,1},{1,2},{2,3},{3,4},{4,5},{5,6},{6,7},{7,8},{8,9},{9,10},{10,1... | collective-permute-start | bytes 1572872 | tf_op jit(solution)/shard_map/while/body/eval_jaxpr/ppermute | solution.py:17
  537.5 15.5 %collective-permute-start.1 = (bf16[16,128,128]{2,1,0:T(8,128)(2,1)}, bf16[16,128,128]{2,1,0:T(8,128)(2,1)S(1)}, u32[]{:S(2)}, u32[]{:S(2)}) collective-permute-start(bf16[16,128,128]{2,1,0:T(8,128)(2,1)} %get-tuple-element.485), channel_id=1, source_target_pairs={{0,1},{1,2},{2,3},{3,4},{4,5},{5,6},{6,7},{7,8},{8,9},{9,10},{10,1... | collective-permute-start | bytes 1572872 | tf_op jit(solution)/shard_map/while/body/eval_jaxpr/ppermute | solution.py:17
  570.4 15.5 %collective-permute-start.1 = (bf16[16,128,128]{2,1,0:T(8,128)(2,1)}, bf16[16,128,128]{2,1,0:T(8,128)(2,1)S(1)}, u32[]{:S(2)}, u32[]{:S(2)}) collective-permute-start(bf16[16,128,128]{2,1,0:T(8,128)(2,1)} %get-tuple-element.485), channel_id=1, source_target_pairs={{0,1},{1,2},{2,3},{3,4},{4,5},{5,6},{6,7},{7,8},{8,9},{9,10},{10,1... | collective-permute-start | bytes 1572872 | tf_op jit(solution)/shard_map/while/body/eval_jaxpr/ppermute | solution.py:17
  603.2 15.5 %collective-permute-start.1 = (bf16[16,128,128]{2,1,0:T(8,128)(2,1)}, bf16[16,128,128]{2,1,0:T(8,128)(2,1)S(1)}, u32[]{:S(2)}, u32[]{:S(2)}) collective-permute-start(bf16[16,128,128]{2,1,0:T(8,128)(2,1)} %get-tuple-element.485), channel_id=1, source_target_pairs={{0,1},{1,2},{2,3},{3,4},{4,5},{5,6},{6,7},{7,8},{8,9},{9,10},{10,1... | collective-permute-start | bytes 1572872 | tf_op jit(solution)/shard_map/while/body/eval_jaxpr/ppermute | solution.py:17
  (34 other events, 268.9 us)
where the time goes:
time: 677 us; the launch traced here: 669 us
  local copies, waits for them, and re-layouts  180 us (27%)
  matrix products  161 us (24%)
  starting transfers between devices  134 us (20%)
  other arithmetic  105 us (16%)
  waiting for transfers between devices  63.5 us (9%)
  blocking collectives  21.4 us (3%)
    ppermute x30, starting transfers between devices, shifted(): return lax.ppermute(value, axis, pairs)  112 us
    dot_general x17, matrix products, tile_terms(): jnp.einsum('...qk,...kd->...qd', rounded, value_tiles, preferred_element_...  106 us
    ppermute x30, waiting for transfers between devices, shifted(): return lax.ppermute(value, axis, pairs)  63.5 us
    unnamed x4, other arithmetic  56.2 us
    dot_general x16, matrix products, span_terms(): jnp.einsum('hrqd,hrskd->hrsqk', q_tiles, picked_k, preferred_element_type...  54.8 us
    gather x17, local copies, waits for them, and re-layouts, span_terms(): picked_k = jnp.take(key_tiles, index, axis=0)  47.7 us
    gather x17, local copies, waits for them, and re-layouts, span_terms(): picked_v = jnp.take(val_tiles, index, axis=0)  47 us
    while x75, local copies, waits for them, and re-layouts  36.1 us
  transfers between devices with their start and end apart: 33, of which 15 were waited for; matrix products, arithmetic and copies ran while one was open for 30% of the time, Pallas kernels for 0%

commit v1 on v0

v1 whole, which is shorter than its diff:
```python
import functools
import math

import jax
import jax.numpy as jnp
from jax import lax
from jax.experimental import pallas as pl
from jax.experimental.pallas import tpu as pltpu
from jax.sharding import PartitionSpec as P

HD = 128
BLOCK = 128
SLOTS = 3
NB = 16
SPANS = 16
RING = 8
UNROLL = 8
F32 = jnp.float32
BF16 = jnp.bfloat16
LOW = -1e30
OFF = 2e30
SCALE = HD ** (-0.5) * math.log2(math.e)
MESH = pl.DeviceIdType.MESH

ZB = 16
XB = NB - ZB


def dot(a, b):
    return jnp.dot(a, b, preferred_element_type=F32)


def kernel(q_hbm, k_hbm, v_ref, b_hbm, out_ref, *scratch):
    kv = [[scratch[s * 2 + t] for t in range(2)] for s in range(RING)]
    (vt, qbuf, qt, obuf, acc, m_ref, l_ref, lst_v, lst, sem_own, sem_send, sem_o,
     rz, sz, rs, ss, sem_l) = scratch[2 * RING:]
    h = lax.axis_index("head")
    c = lax.axis_index("blk")
    z, core = c // 2, c % 2
    mirror = SPANS - 1 - c
    sib = (h, 2 * z + 1 - core)
    up = (h, lax.rem(c + 2, SPANS))
    down = (h, lax.rem(c + SPANS - 2, SPANS))

    def wait(ref, sem):
        pltpu.make_async_copy(ref, ref, sem).wait()

    def send(src, dst, s_sem, r_sem, dev):
        pltpu.make_async_remote_copy(
            src_ref=src, dst_ref=dst, send_sem=s_sem, recv_sem=r_sem,
            device_id=dev, device_id_type=MESH).start()

    barrier = pltpu.get_barrier_semaphore()

    def hello(dev):
        pl.semaphore_signal(barrier, inc=1, device_id=dev, device_id_type=MESH)

    def greet(j, _):
        hello((lax.rem(h + j, NB), c))
        return 0

    lax.fori_loop(1, NB, greet, 0)

    def greet_mirror(j, _):
        hello((lax.rem(h + j, NB), mirror))
        return 0

    lax.fori_loop(0, NB, greet_mirror, 0)
    hello(sib)
    hello(up)
    hello(down)

    for g in range(8):
        vt[g] = v_ref[:, g * HD:(g + 1) * HD].T
    pl.semaphore_wait(barrier, 34)

    mine = kv[0][0]

    def send_k(j, _):
        p = lax.rem(h + j, NB)
        col = pl.multiple_of((p // 2) * HD, HD)
        send(k_hbm.at[:, pl.ds(col, HD)], mine.at[h], sem_send.at[0], sem_own.at[0], (p, c))
        return 0

    lax.fori_loop(1, NB, send_k, 0)
    own_col = pl.multiple_of((h // 2) * HD, HD)
    pltpu.make_async_copy(k_hbm.at[:, pl.ds(own_col, HD)], mine.at[h], sem_own.at[0]).start()

    def send_v(j, _):
        p = lax.rem(h + j, NB)
        send(vt.at[p // 2], mine.at[NB + h], sem_send.at[1], sem_own.at[1], (p, c))
        return 0

    lax.fori_loop(1, NB, send_v, 0)
    pltpu.make_async_copy(vt.at[h // 2], mine.at[NB + h], sem_own.at[1]).start()

    def q_cols(p, i):
        return pl.ds(pl.multiple_of((2 * p + i) * HD, HD), HD)

    near = lax.rem(h, 2)
    far = 1 - near

    def send_q_near(j, _):
        p = lax.rem(h + j, NB)
        send(q_hbm.at[:, q_cols(p, near)], qbuf.at[0, h], sem_send.at[2], sem_own.at[2], (p, c))
        return 0

    lax.fori_loop(1, NB, send_q_near, 0)
    pltpu.make_async_copy(q_hbm.at[:, q_cols(h, near)], qbuf.at[0, h], sem_own.at[2]).start()

    def send_q_far(j, _):
        p = lax.rem(h + j, NB)
        send(q_hbm.at[:, q_cols(p, far)], qbuf.at[1, h], sem_send.at[3], sem_own.at[3], (p, mirror))
        return 0

    lax.fori_loop(0, NB, send_q_far, 0)

    send(b_hbm, lst_v, sem_l.at[0], sem_l.at[1], (h, mirror))
    pltpu.make_async_copy(b_hbm, lst.at[0], sem_l.at[2]).start()

    def part(s, t, which, first=0, count=NB):
        return kv[s][t].at[pl.ds(which * NB + first, count)]

    def go_up(s, which):
        send(part(s, 0, which), part(s + 1, 0, which), sz.at[0, s, which],
             rz.at[s + 1, which], up)

    def go_down(s, which):
        d = s if s else RING
        send(part(s, 0, which), part(d - 1, 0, which), sz.at[1, s, which],
             rz.at[d - 1, which], down)

    def go_side(s, which):
        send(part(s, 0, which), part(s, 1, which), ss.at[s, which], rs.at[s, which], sib)

    def got(s, which):
        wait(part(s, 0, which), rz.at[s, which])

    def got_side(s):
        for which in range(2):
            wait(part(s, 1, which), rs.at[s, which])

    def span_of(s, t):
        zz = lax.rem(z + RING - s, RING)
        return 2 * zz + (core if t == 0 else 1 - core)

    def row(r):
        group = r // NB
        return group, lax.rem(r, NB)

    def absorb(r, parts, value_tiles):
        m_old = m_ref[r]
        top = m_old
        for s, off in parts:
            top = jnp.maximum(top, jnp.max(s, axis=0, keepdims=True) * SCALE - off)
        keep = jnp.exp2(m_old - top)
        probs = [jnp.exp2(s * SCALE - (top + off)) for s, off in parts]
        total = jnp.sum(functools.reduce(jnp.add, probs), axis=0, keepdims=True)
        out = None
        for p, tile in zip(probs, value_tiles):
            o = dot(tile, p.astype(BF16))
            out = o if out is None else out + o
        acc[r] = acc[r] * keep + out
        l_ref[r] = l_ref[r] * keep + total
        m_ref[r] = top

    def compute(s, t):
        ref = kv[s][t]
        span = span_of(s, t)
        lo = jnp.where(span <= c, 0, NB // UNROLL)
        hi = jnp.where(span <= mirror, 2 * NB // UNROLL, NB // UNROLL)

        def some(it, _):
            for u in range(UNROLL):
                r = it * UNROLL + u
                group, b = row(r)
                i = lax.rem(u + group, 2)
                limit = jnp.where(span < jnp.where(group == 0, c, mirror), NB, b)
                parts, tiles = [], []
                for j in range(SLOTS):
                    e = lst[group, i, b, span * SLOTS + j]
                    off = jnp.where((e >= 0) & (e < limit), 0.0, OFF)
                    at = jnp.clip(e, 0, NB - 1)
                    parts.append((dot(ref[at], qt[r]), off))
                    tiles.append(ref[NB + at])
                absorb(r, parts, tiles)
            return 0

        lax.fori_loop(lo, hi, some, 0)

    def diagonal(s, t, group):
        ref = kv[s][t]

        def some(it, _):
            keys = lax.broadcasted_iota(jnp.int32, (BLOCK, BLOCK), 0)
            toks = lax.broadcasted_iota(jnp.int32, (BLOCK, BLOCK), 1)
            for u in range(4):
                b = it * 4 + u
                r = group * NB + b
                scores = jnp.where(keys <= toks, dot(ref[b], qt[r]), LOW)
                absorb(r, [(scores, 0.0)], [ref[NB + b]])
            return 0

        lax.fori_loop(0, NB // 4, some, 0)

    wait(part(0, 0, 0), sem_own.at[0])
    go_up(0, 0)
    go_down(0, 0)
    go_side(0, 0)
    wait(part(0, 0, 1), sem_own.at[1])
    go_up(0, 1)
    go_down(0, 1)
    go_side(0, 1)

    def init(r, _):
        acc[r] = jnp.zeros((HD, BLOCK), F32)
        m_ref[r] = jnp.full((1, BLOCK), LOW, F32)
        l_ref[r] = jnp.zeros((1, BLOCK), F32)
        return 0

    lax.fori_loop(0, 2 * NB, init, 0)

    def turn(group):
        def one(b, _):
            qt[group * NB + b] = qbuf[group, b].T
            return 0

        lax.fori_loop(0, NB, one, 0)

    wait(qbuf.at[0], sem_own.at[2])
    turn(0)
    diagonal(0, 0, 0)
    wait(qbuf.at[1], sem_own.at[3])
    turn(1)
    wait(lst_v, sem_l.at[1])
    pltpu.make_async_copy(lst_v, lst.at[1], sem_l.at[3]).start()
    pltpu.make_async_copy(b_hbm, lst.at[0], sem_l.at[2]).wait()
    pltpu.make_async_copy(lst_v, lst.at[1], sem_l.at[3]).wait()

    mirror_at = lax.rem(2 * z + 1, RING)

    def step(s, t):
        if t == 1:
            got_side(s)
        compute(s, t)
        if t == 1 and s % 2 == 1:
            @pl.when(mirror_at == s)
            def _():
                diagonal(s, t, 1)

    def poll(s_up, s_down, which):
        got(s_up, which)
        if s_up < 3 or (s_up == 3 and which == 0):
            go_up(s_up, which)
        got(s_down, which)
        if s_down > 5 or (s_down == 5 and which == 1):
            go_down(s_down, which)
        go_side(s_up, which)
        go_side(s_down, which)

    step(0, 0)
    poll(1, 7, 0)
    step(0, 1)
    poll(1, 7, 1)
    step(1, 0)
    step(7, 0)
    poll(2, 6, 0)
    step(1, 1)
    step(7, 1)
    poll(2, 6, 1)
    step(2, 0)
    step(6, 0)
    poll(3, 5, 0)
    step(2, 1)
    step(6, 1)
    poll(3, 5, 1)
    step(3, 0)
    step(5, 0)
    step(3, 1)
    step(5, 1)
    for which in range(2):
        got(4, which)
        go_side(4, which)
    step(4, 0)
    step(4, 1)

    def out_cols(i):
        return pl.ds(pl.multiple_of((2 * h + i) * HD, HD), HD)

    def finish(b, group):
        r = group * NB + b
        obuf[r] = (acc[r] / l_ref[r]).T.astype(BF16)
        i = lax.rem(b + group, 2)
        return obuf.at[r], out_ref.at[:, out_cols(i)]

    def finish_far(j, _):
        b = lax.rem(h + j, NB)
        src, dst = finish(b, 1)
        send(src, dst, sem_o.at[0], sem_o.at[1], (b, mirror))
        return 0

    lax.fori_loop(0, NB, finish_far, 0)

    def finish_near(j, _):
        b = lax.rem(h + j, NB)
        src, dst = finish(b, 0)
        send(src, dst, sem_o.at[0], sem_o.at[1], (b, c))
        return 0

    lax.fori_loop(1, NB, finish_near, 0)
    src, dst = finish(h, 0)
    pltpu.make_async_copy(src, dst, sem_o.at[1]).start()
    wait(out_ref, sem_o.at[1])

    wait(mine.at[pl.ds(0, NB - 1)], sem_send.at[0])
    wait(mine.at[pl.ds(0, NB - 1)], sem_send.at[1])
    wait(qbuf.at[0, pl.ds(0, NB - 1)], sem_send.at[2])
    wait(qbuf.at[1], sem_send.at[3])
    wait(lst_v, sem_l.at[0])
    wait(obuf.at[pl.ds(0, 2 * NB - 1)], sem_o.at[0])
    for s in range(RING):
        for which in range(2):
            wait(part(s, 0, which), ss.at[s, which])
            if s < 3 or (s == 3 and which == 0):
                wait(part(s, 0, which), sz.at[0, s, which])
            if s == 0 or s > 5 or (s == 5 and which == 1):
                wait(part(s, 0, which), sz.at[1, s, which])


def body(queries, keys, values, blocks):
    anywhere = pl.BlockSpec(memory_space=pl.ANY)
    vmem = pl.BlockSpec(memory_space=pltpu.VMEM)
    dma = pltpu.SemaphoreType.DMA
    out = pl.pallas_call(
        kernel,
        out_shape=jax.ShapeDtypeStruct((BLOCK, queries.shape[2]), BF16),
        in_specs=[anywhere, anywhere, vmem, anywhere],
        out_specs=vmem,
        scratch_shapes=[pltpu.VMEM((2 * NB, BLOCK, HD), BF16) for _ in range(2 * RING)] + [
            pltpu.VMEM((8, HD, BLOCK), BF16),
            pltpu.VMEM((2, NB, BLOCK, HD), BF16),
            pltpu.VMEM((2 * NB, HD, BLOCK), BF16),
            pltpu.VMEM((2 * NB, BLOCK, HD), BF16),
            pltpu.VMEM((2 * NB, HD, BLOCK), F32),
            pltpu.VMEM((2 * NB, 1, BLOCK), F32),
            pltpu.VMEM((2 * NB, 1, BLOCK), F32),
            pltpu.VMEM((2, NB, SPANS * SLOTS), jnp.int32),
            pltpu.SMEM((2, 2, NB, SPANS * SLOTS), jnp.int32),
            dma((4,)),
            dma((4,)),
            dma((2,)),
            dma((RING, 2)),
            dma((2, RING, 2)),
            dma((RING, 2)),
            dma((RING, 2)),
            dma((4,)),
        ],
        compiler_params=pltpu.CompilerParams(
            collective_id=0, has_side_effects=True, vmem_limit_bytes=48 * 2**20),
        name="attend",
    )(queries[0], keys[0], values[0], blocks[:, 0])
    return out[None]


def solution(mesh):
    placed = (
        P("blk", "head", None),
        P("blk", "head", None),
        P("blk", "head", None),
        P("head", "blk", None, None),
    )
    return jax.shard_map(
        body, mesh=mesh, in_specs=placed, out_specs=P("blk", "head", None), check_vma=False
    )
```

time: 677 us -> 164 us (0.24)
  the two profiles are of different devices: /device:TPU:97 before, /device:TPU:1 now
where the time goes in v1:
time: 164 us
  Pallas kernels  159 us (97%)
  local copies, waits for them, and re-layouts  4.81 us (3%)
    pallas_call x1, Pallas kernels, body(): pl.pallas_call(kernel, out_shape=jax.ShapeDtypeStruct((BLOCK, queries.sha...  159 us
    unnamed x9, local copies, waits for them, and re-layouts  4.81 us

profile of v1, /device:TPU:1, one launch (start us, length us, event | category | flops | bytes accessed | tf_op | source)
XLA Modules:
  0.0 163.9 jit_solution(13559588451908166758)
XLA Ops:
  0.0 0.0 copy-start
  0.0 1.2 copy-done
  1.2 0.0 copy-start.1
  1.2 0.9 copy-done.1
  2.2 0.0 copy-start.2
  2.2 0.9 copy-done.2
  3.1 0.0 copy-start.3
  3.1 0.7 copy-done.3
  3.8 159.1 %attend.1 = bf16[128,4096]{1,0:T(8,128)(2,1)S(1)} custom-call(bf16[128,4096]{1,0:T(8,128)(2,1)S(1)} %bitcast.6, bf16[128,1024]{1,0:T(8,128)(2,1)S(1)} %bitcast.7, bf16[128,1024]{1,0:T(8,128)(2,1)S(1)} %bitcast.8, s32[2,16,48]{2,1,0:T(8,128)S(1)} %bitcast.9), custom_call_target="tpu_custom_call" | custom-call | tf_op jit(solution)/shard_map/attend/pallas_call | solution.py:334
  162.9 1.0 copy.6
Async XLA Ops:
  0.0 1.2 copy-start
  1.2 0.9 copy-start.1
  2.2 0.9 copy-start.2
  3.1 0.7 copy-start.3

commit v2 on v0

v2 whole, which is shorter than its diff:
```python
import functools
import math

import jax
import jax.numpy as jnp
from jax import lax
from jax.experimental import pallas as pl
from jax.experimental.pallas import tpu as pltpu
from jax.sharding import PartitionSpec as P

HD = 128
BLOCK = 128
SLOTS = 3
NB = 16
SPANS = 16
PAIRS = 8
SIDE = 4
F32 = jnp.float32
BF16 = jnp.bfloat16
LOW = -1e30
OFF = 2e30
SCALE = HD ** (-0.5) * math.log2(math.e)
MESH = pl.DeviceIdType.MESH


def dot(a, b):
    return jnp.dot(a, b, preferred_element_type=F32)


def kernel(q_hbm, k_hbm, v_ref, b_ref, out_ref, *scratch):
    kv = [[scratch[j * 2 + t] for t in range(2)] for j in range(PAIRS)]
    (vt, own, qbuf, qt, obuf, acc, m_ref, l_ref, lists, lst_v, lst,
     sem_own, sem_kvs, sem_q, sem_qs, sem_o, sem_l, sem_cp,
     r1, r2, r3, r4, rs, s1, s2, s3, s4, ss) = scratch[2 * PAIRS:]
    h = lax.axis_index("head")
    c = lax.axis_index("blk")
    z, core = c // 2, c % 2
    x, y = h % SIDE, h // SIDE
    sib = (h, 2 * z + 1 - core)
    a = jnp.where(core == 0, x, y)
    b = jnp.where(core == 0, y, x)
    place = b * SIDE + a
    mirrored = a * SIDE + b

    def device(aa, bb):
        aa, bb = lax.rem(aa, SIDE), lax.rem(bb, SIDE)
        return (jnp.where(core == 0, bb * SIDE + aa, aa * SIDE + bb), c)

    a_next, a_prev = device(a + 1, b), device(a + SIDE - 1, b)
    b_next, b_prev = device(a, b + 1), device(a, b + SIDE - 1)

    def wait(ref, sem):
        pltpu.make_async_copy(ref, ref, sem).wait()

    def send(src, dst, s_sem, r_sem, dev):
        pltpu.make_async_remote_copy(
            src_ref=src, dst_ref=dst, send_sem=s_sem, recv_sem=r_sem,
            device_id=dev, device_id_type=MESH).start()

    barrier = pltpu.get_barrier_semaphore()

    def hello(dev):
        pl.semaphore_signal(barrier, inc=1, device_id=dev, device_id_type=MESH)

    def greet(j, _):
        other = lax.rem(c + j, SPANS)
        hello((h, other))
        hello((c, other))
        return 0

    lax.fori_loop(1, SPANS, greet, 0)
    for dev in (a_next, a_prev, b_next, b_prev):
        hello(dev)

    @pl.when(c != h)
    def _():
        hello((c, c))

    for g in range(PAIRS):
        vt[g] = v_ref[:, g * HD:(g + 1) * HD].T
    lists[...] = jnp.zeros(lists.shape, jnp.int32)
    for n in range(NB):
        lists[n, 0:2, 0:SPANS * SLOTS] = b_ref[:, n, :]
    pl.semaphore_wait(barrier, 34 + jnp.where(c != h, 1, 0))

    def chip(n):
        away = jnp.where(n % 2 == 1, (n + 1) // 2, PAIRS - n // 2)
        return lax.rem(z + away, PAIRS)

    def key_cols(g):
        return pl.ds(pl.multiple_of(g * HD, HD), HD)

    def send_kv(n, _):
        g = chip(n)
        send(k_hbm.at[:, key_cols(g)], own.at[z, 0], sem_kvs.at[0], sem_own.at[z], (h, 2 * g + core))
        send(vt.at[g], own.at[z, 1], sem_kvs.at[1], sem_own.at[z], (h, 2 * g + core))
        return 0

    lax.fori_loop(1, PAIRS, send_kv, 0)
    pltpu.make_async_copy(k_hbm.at[:, key_cols(z)], own.at[z, 0], sem_own.at[z]).start()
    pltpu.make_async_copy(vt.at[z], own.at[z, 1], sem_own.at[z]).start()

    def send_list(j, _):
        p = lax.rem(h + j, NB)
        send(lists.at[p], lst_v.at[c], sem_l.at[0], sem_l.at[1], (p, h))
        return 0

    lax.fori_loop(1, NB, send_list, 0)

    @pl.when(c != h)
    def _():
        send(lists.at[h], lst_v.at[c], sem_l.at[2], sem_l.at[1], (h, h))

    @pl.when(c == h)
    def _():
        pltpu.make_async_copy(lists.at[h], lst_v.at[c], sem_l.at[1]).start()

    def q_cols(p):
        return pl.ds(pl.multiple_of(p * 2 * HD, 2 * HD), 2 * HD)

    def send_q(p):
        send(q_hbm.at[:, q_cols(p)], qbuf.at[c], sem_qs.at[0], sem_q.at[c], (h, p))

    pltpu.make_async_copy(q_hbm.at[:, q_cols(c)], qbuf.at[c], sem_q.at[c]).start()
    send_q(2 * z + 1 - core)

    def send_qs(n, _):
        g = chip(n)
        send_q(2 * g)
        send_q(2 * g + 1)
        return 0

    lax.fori_loop(1, PAIRS, send_qs, 0)

    def line(j, t, bb):
        return kv[j][t].at[pl.ds(lax.rem(bb, SIDE) * SIDE, SIDE)]

    def half(j, bb, which):
        return kv[j][0].at[pl.ds(lax.rem(bb, SIDE) * SIDE, SIDE), which]

    def tile(j, aa):
        return kv[j][0].at[b * SIDE + lax.rem(aa, SIDE)]

    def tile_half(j, aa, which):
        return kv[j][0].at[b * SIDE + lax.rem(aa, SIDE), which]

    def aside(j, bb):
        send(line(j, 0, bb), line(j, 1, bb), ss.at[j], rs.at[j], sib)

    def event1(j):
        wait(own.at[j], sem_own.at[j])
        send(own.at[j], kv[j][0].at[place], s1.at[j, 0], r1.at[j, 0], a_next)
        send(own.at[j], kv[j][0].at[place], s1.at[j, 1], r1.at[j, 1], a_prev)
        pltpu.make_async_copy(own.at[j], kv[j][0].at[place], sem_cp.at[j]).start()

    def event2(j):
        wait(tile(j, a + 3), r1.at[j, 0])
        send(tile_half(j, a + 3, 0), tile_half(j, a + 3, 0), s2.at[j, 0], r2.at[j, 0], a_next)
        wait(tile(j, a + 1), r1.at[j, 1])
        send(tile_half(j, a + 1, 1), tile_half(j, a + 1, 1), s2.at[j, 1], r2.at[j, 1], a_prev)

    def event3(j):
        wait(tile_half(j, a + 2, 0), r2.at[j, 0])
        wait(tile_half(j, a + 2, 1), r2.at[j, 1])
        wait(kv[j][0].at[place], sem_cp.at[j])
        send(line(j, 0, b), line(j, 0, b), s3.at[j, 0], r3.at[j, 0], b_next)
        send(line(j, 0, b), line(j, 0, b), s3.at[j, 1], r3.at[j, 1], b_prev)
        aside(j, b)

    def event4(j):
        wait(line(j, 0, b + 3), r3.at[j, 0])
        send(half(j, b + 3, 0), half(j, b + 3, 0), s4.at[j, 0], r4.at[j, 0], b_next)
        wait(line(j, 0, b + 1), r3.at[j, 1])
        send(half(j, b + 1, 1), half(j, b + 1, 1), s4.at[j, 1], r4.at[j, 1], b_prev)
        aside(j, b + 3)
        aside(j, b + 1)

    def event5(j):
        wait(half(j, b + 2, 0), r4.at[j, 0])
        wait(half(j, b + 2, 1), r4.at[j, 1])
        aside(j, b + 2)

    def events(n):
        for late, event in enumerate((event1, event2, event3, event4, event5)):
            if 0 <= n - late < PAIRS:
                event(n - late)

    parity = (core, 1 - core)

    def tiles_of(j, cc, i):
        parts = []
        for t in range(2):
            span = 2 * j + parity[t]
            limit = jnp.where(span < cc, NB, jnp.where(span == cc, h, 0))
            for n in range(SLOTS):
                e = lst[cc, i, span * SLOTS + n]
                off = jnp.where((e >= 0) & (e < limit), 0.0, OFF)
                e = jnp.clip(e, 0, NB - 1)
                at = jnp.where(parity[t] == 0, e, (e % SIDE) * SIDE + e // SIDE)
                scores = dot(kv[j][t][at, 0], qt[cc, i])
                parts.append((scores, off, kv[j][t][at, 1]))
        return parts

    def absorb(cc, i, parts, first):
        top = jnp.full((1, BLOCK), LOW, F32) if first else m_ref[cc, i]
        m_old = top
        for s, off, _ in parts:
            top = jnp.maximum(top, jnp.max(s, axis=0, keepdims=True) * SCALE - off)
        probs = [jnp.exp2(s * SCALE - (top + off)) for s, off, _ in parts]
        total = jnp.sum(functools.reduce(jnp.add, probs), axis=0, keepdims=True)
        out = None
        for p, (_, _, values) in zip(probs, parts):
            o = dot(values, p.astype(BF16))
            out = o if out is None else out + o
        if not first:
            keep = jnp.exp2(m_old - top)
            total = l_ref[cc, i] * keep + total
            out = acc[cc, i] * keep + out
        return top, total, out

    def later_rows(j, pair):
        for u in range(2):
            for i in range(2):
                cc = 2 * pair + u
                top, total, out = absorb(cc, i, tiles_of(j, cc, i), j == 0)
                m_ref[cc, i] = top
                l_ref[cc, i] = total
                acc[cc, i] = out

    def out_cols(p):
        return pl.ds(pl.multiple_of(p * 2 * HD, 2 * HD), 2 * HD)

    def last_rows(j):
        keys = lax.broadcasted_iota(jnp.int32, (BLOCK, BLOCK), 0)
        toks = lax.broadcasted_iota(jnp.int32, (BLOCK, BLOCK), 1)
        for t in range(2):
            cc = 2 * j + parity[t]
            here = place if t == 0 else mirrored
            for i in range(2):
                scores = jnp.where(keys <= toks, dot(kv[j][t][here, 0], qt[cc, i]), LOW)
                parts = tiles_of(j, cc, i) + [(scores, 0.0, kv[j][t][here, 1])]
                _, total, out = absorb(cc, i, parts, j == 0)
                obuf[cc, :, i * HD:(i + 1) * HD] = (out / total).T.astype(BF16)
        for t in range(2):
            cc = 2 * j + parity[t]

            @pl.when(cc != c)
            def _():
                send(obuf.at[cc], out_ref.at[:, out_cols(c)], sem_o.at[0], sem_o.at[1], (h, cc))

            @pl.when(cc == c)
            def _():
                pltpu.make_async_copy(obuf.at[cc], out_ref.at[:, out_cols(c)], sem_o.at[1]).start()

    def turn(cc):
        wait(qbuf.at[cc], sem_q.at[cc])
        for i in range(2):
            qt[cc, i] = qbuf[cc, :, i * HD:(i + 1) * HD].T

    for n in range(5):
        events(n)
    wait(lst_v, sem_l.at[1])
    pltpu.make_async_copy(lst_v, lst, sem_l.at[3]).start()
    pltpu.make_async_copy(lst_v, lst, sem_l.at[3]).wait()

    plan = {0: {1: 5, 4: 6, 6: 7}, 1: {1: 8, 3: 9, 5: 10}, 2: {1: 11}}
    for j in range(PAIRS):
        wait(kv[j][1], rs.at[j])
        marks = plan.get(j, {})
        if j == 0:
            def some(n, _):
                pair = chip(n)
                turn(2 * pair)
                turn(2 * pair + 1)

                @pl.when(pair != 0)
                def _():
                    later_rows(0, pair)

                for at, step in marks.items():
                    @pl.when(n == at)
                    def _():
                        events(step)
                return 0

            lax.fori_loop(0, PAIRS, some, 0)
            last_rows(0)
        else:
            last_rows(j)
            if j + 1 < PAIRS:
                def some(pair, _):
                    later_rows(j, pair)
                    for at, step in marks.items():
                        @pl.when(pair == j + at)
                        def _():
                            events(step)
                    return 0

                lax.fori_loop(j + 1, PAIRS, some, 0)

    wait(out_ref, sem_o.at[1])

    wait(own.at[pl.ds(0, PAIRS - 1), 0], sem_kvs.at[0])
    wait(own.at[pl.ds(0, PAIRS - 1), 1], sem_kvs.at[1])
    wait(lists.at[pl.ds(0, NB - 1)], sem_l.at[0])

    @pl.when(c != h)
    def _():
        wait(lists.at[0], sem_l.at[2])

    wait(qbuf.at[pl.ds(0, SPANS - 1)], sem_qs.at[0])
    wait(obuf.at[pl.ds(0, SPANS - 1)], sem_o.at[0])
    for j in range(PAIRS):
        for n in range(2):
            wait(own.at[j], s1.at[j, n])
            wait(tile_half(j, a, n), s2.at[j, n])
            wait(line(j, 0, b), s3.at[j, n])
            wait(half(j, b, n), s4.at[j, n])
        wait(kv[j][0], ss.at[j])


def body(queries, keys, values, blocks):
    anywhere = pl.BlockSpec(memory_space=pl.ANY)
    vmem = pl.BlockSpec(memory_space=pltpu.VMEM)
    dma = pltpu.SemaphoreType.DMA
    events = [dma((PAIRS, 2)) for _ in range(4)] + [dma((PAIRS,))]
    out = pl.pallas_call(
        kernel,
        out_shape=jax.ShapeDtypeStruct((BLOCK, queries.shape[2]), BF16),
        in_specs=[anywhere, anywhere, vmem, vmem],
        out_specs=vmem,
        scratch_shapes=[pltpu.VMEM((NB, 2, BLOCK, HD), BF16) for _ in range(2 * PAIRS)] + [
            pltpu.VMEM((PAIRS, HD, BLOCK), BF16),
            pltpu.VMEM((PAIRS, 2, BLOCK, HD), BF16),
            pltpu.VMEM((SPANS, BLOCK, 2 * HD), BF16),
            pltpu.VMEM((SPANS, 2, HD, BLOCK), BF16),
            pltpu.VMEM((SPANS, BLOCK, 2 * HD), BF16),
            pltpu.VMEM((SPANS, 2, HD, BLOCK), F32),
            pltpu.VMEM((SPANS, 2, 1, BLOCK), F32),
            pltpu.VMEM((SPANS, 2, 1, BLOCK), F32),
            pltpu.VMEM((NB, 8, 128), jnp.int32),
            pltpu.VMEM((SPANS, 8, 128), jnp.int32),
            pltpu.SMEM((SPANS, 8, 128), jnp.int32),
            dma((PAIRS,)),
            dma((2,)),
            dma((SPANS,)),
            dma((1,)),
            dma((2,)),
            dma((4,)),
            dma((PAIRS,)),
        ] + events + events,
        compiler_params=pltpu.CompilerParams(
            collective_id=0, has_side_effects=True, vmem_limit_bytes=48 * 2**20),
        name="attend",
    )(queries[0], keys[0], values[0], blocks[:, 0])
    return out[None]


def solution(mesh):
    placed = (
        P("blk", "head", None),
        P("blk", "head", None),
        P("blk", "head", None),
        P("head", "blk", None, None),
    )
    return jax.shard_map(
        body, mesh=mesh, in_specs=placed, out_specs=P("blk", "head", None), check_vma=False
    )
```

time: 677 us -> 116 us (0.17)
  the two profiles are of different devices: /device:TPU:97 before, /device:TPU:225 now
where the time goes in v2:
time: 116 us; the launch traced here: 115 us
  Pallas kernels  111 us (96%)
  local copies, waits for them, and re-layouts  4.81 us (4%)
    pallas_call x1, Pallas kernels, body(): pl.pallas_call(kernel, out_shape=jax.ShapeDtypeStruct((BLOCK, queries.sha...  111 us
    unnamed x9, local copies, waits for them, and re-layouts  4.81 us

profile of v2, /device:TPU:225, one launch (start us, length us, event | category | flops | bytes accessed | tf_op | source)
XLA Modules:
  0.0 115.4 jit_solution(3715964865494836539)
XLA Ops:
  0.0 0.0 copy-start
  0.0 1.2 %copy-done = bf16[1,128,4096]{2,1,0:T(8,128)(2,1)S(1)} copy-done((bf16[1,128,4096]{2,1,0:T(8,128)(2,1)S(1)}, bf16[1,128,4096]{2,1,0:T(8,128)(2,1)}, u32[]{:S(2)}) %copy-start) | copy-done | bytes 1048600
  1.2 0.0 copy-start.1
  1.2 0.9 copy-done.1
  2.2 0.0 copy-start.2
  2.2 0.9 copy-done.2
  3.1 0.0 copy-start.3
  3.1 0.7 copy-done.3
  3.8 110.6 %attend.1 = bf16[128,4096]{1,0:T(8,128)(2,1)S(1)} custom-call(bf16[128,4096]{1,0:T(8,128)(2,1)S(1)} %bitcast.6, bf16[128,1024]{1,0:T(8,128)(2,1)S(1)} %bitcast.7, bf16[128,1024]{1,0:T(8,128)(2,1)S(1)} %bitcast.8, s32[2,16,48]{2,1,0:T(8,128)S(1)} %bitcast.9), custom_call_target="tpu_custom_call" | custom-call | tf_op jit(solution)/shard_map/attend/pallas_call | solution.py:327
  114.4 1.0 copy.6
Async XLA Ops:
  0.0 1.2 %copy-start = (bf16[1,128,4096]{2,1,0:T(8,128)(2,1)S(1)}, bf16[1,128,4096]{2,1,0:T(8,128)(2,1)}, u32[]{:S(2)}) copy-start(bf16[1,128,4096]{2,1,0:T(8,128)(2,1)} %param.4) | copy-start | bytes 3145732
  1.2 0.9 copy-start.1
  2.2 0.9 copy-start.2
  3.1 0.7 copy-start.3

commit v3 on v2

--- a/solution.py
+++ b/solution.py
@@ -263,7 +263,7 @@
     pltpu.make_async_copy(lst_v, lst, sem_l.at[3]).start()
     pltpu.make_async_copy(lst_v, lst, sem_l.at[3]).wait()
 
-    plan = {0: {1: 5, 4: 6, 6: 7}, 1: {1: 8, 3: 9, 5: 10}, 2: {1: 11}}
+    plan = {j: {1: 5 + j} for j in range(7)}
     for j in range(PAIRS):
         wait(kv[j][1], rs.at[j])
         marks = plan.get(j, {})
@@ -350,7 +350,7 @@
             dma((PAIRS,)),
         ] + events + events,
         compiler_params=pltpu.CompilerParams(
-            collective_id=0, has_side_effects=True, vmem_limit_bytes=48 * 2**20),
+            collective_id=0, has_side_effects=True, vmem_limit_bytes=60 * 2**20),
         name="attend",
     )(queries[0], keys[0], values[0], blocks[:, 0])
     return out[None]

time: 116 us -> 106 us (0.914)
  Pallas kernels: 111 us -> 104 us
  local copies, waits for them, and re-layouts: 4.81 us -> 2.29 us
    pallas_call x1, Pallas kernels: 111 us -> 104 us  [body(): pl.pallas_call(kernel, out_shape=jax.ShapeDtypeStruct((BLOCK, queries.sha...]
    unnamed x9 -> x1, local copies, waits for them, and re-layouts: 4.81 us -> 2.29 us
where the time goes in v3:
time: 106 us
  Pallas kernels  104 us (98%)
  local copies, waits for them, and re-layouts  2.29 us (2%)
    pallas_call x1, Pallas kernels, body(): pl.pallas_call(kernel, out_shape=jax.ShapeDtypeStruct((BLOCK, queries.sha...  104 us
    unnamed x1, local copies, waits for them, and re-layouts  2.29 us

profile of v3, /device:TPU:225, one launch (start us, length us, event | category | flops | bytes accessed | tf_op | source)
XLA Modules:
  0.0 105.9 jit_solution(1789058500508843406)
XLA Ops:
  0.0 103.6 %attend.1 = bf16[128,4096]{1,0:T(8,128)(2,1)} custom-call(bf16[128,4096]{1,0:T(8,128)(2,1)} %bitcast.6, bf16[128,1024]{1,0:T(8,128)(2,1)} %bitcast.7, bf16[128,1024]{1,0:T(8,128)(2,1)} %bitcast.8, s32[2,16,48]{2,1,0:T(8,128)} %bitcast.9), custom_call_target="tpu_custom_call" | custom-call | tf_op jit(solution)/shard_map/attend/pallas_call | solution.py:327
  103.6 2.3 %copy.6 = bf16[1,128,4096]{2,1,0:T(8,128)(2,1)} copy(bf16[1,128,4096]{2,1,0:T(8,128)(2,1)} %bitcast.5) | data formatting | bytes 2097152

commit v4 on v3

--- a/solution.py
+++ b/solution.py
@@ -17,6 +17,7 @@
 SIDE = 4
 F32 = jnp.float32
 BF16 = jnp.bfloat16
+LAGS = (-1, 0, 1, 3, 4)
 LOW = -1e30
 OFF = 2e30
 SCALE = HD ** (-0.5) * math.log2(math.e)
@@ -27,11 +28,11 @@
     return jnp.dot(a, b, preferred_element_type=F32)
 
 
-def kernel(q_hbm, k_hbm, v_ref, b_ref, out_ref, *scratch):
+def kernel(q_hbm, k_hbm, v_hbm, b_hbm, out_ref, *scratch):
     kv = [[scratch[j * 2 + t] for t in range(2)] for j in range(PAIRS)]
-    (vt, own, qbuf, qt, obuf, acc, m_ref, l_ref, lists, lst_v, lst,
+    (v_ref, b_ref, vt, own, qbuf, qt, obuf, acc, m_ref, l_ref, lists, lst_v, lst,
      sem_own, sem_kvs, sem_q, sem_qs, sem_o, sem_l, sem_cp,
-     r1, r2, r3, r4, rs, s1, s2, s3, s4, ss) = scratch[2 * PAIRS:]
+     sem_in, r1, r2, r3, r4, rs, s1, s2, s3, s4, ss) = scratch[2 * PAIRS:]
     h = lax.axis_index("head")
     c = lax.axis_index("blk")
     z, core = c // 2, c % 2
@@ -57,6 +58,11 @@
             src_ref=src, dst_ref=dst, send_sem=s_sem, recv_sem=r_sem,
             device_id=dev, device_id_type=MESH).start()
 
+    fetch_v = pltpu.make_async_copy(v_hbm, v_ref, sem_in.at[0])
+    fetch_b = pltpu.make_async_copy(b_hbm, b_ref, sem_in.at[1])
+    fetch_v.start()
+    fetch_b.start()
+
     barrier = pltpu.get_barrier_semaphore()
 
     def hello(dev):
@@ -76,11 +82,9 @@
     def _():
         hello((c, c))
 
-    for g in range(PAIRS):
-        vt[g] = v_ref[:, g * HD:(g + 1) * HD].T
     lists[...] = jnp.zeros(lists.shape, jnp.int32)
-    for n in range(NB):
-        lists[n, 0:2, 0:SPANS * SLOTS] = b_ref[:, n, :]
+    fetch_v.wait()
+    fetch_b.wait()
     pl.semaphore_wait(barrier, 34 + jnp.where(c != h, 1, 0))
 
     def chip(n):
@@ -90,15 +94,25 @@
     def key_cols(g):
         return pl.ds(pl.multiple_of(g * HD, HD), HD)
 
-    def send_kv(n, _):
+    def send_k(n, _):
         g = chip(n)
         send(k_hbm.at[:, key_cols(g)], own.at[z, 0], sem_kvs.at[0], sem_own.at[z], (h, 2 * g + core))
+        return 0
+
+    def send_v(n, _):
+        g = chip(n)
+        vt[g] = v_ref[:, key_cols(g)].T
         send(vt.at[g], own.at[z, 1], sem_kvs.at[1], sem_own.at[z], (h, 2 * g + core))
         return 0
 
-    lax.fori_loop(1, PAIRS, send_kv, 0)
+    lax.fori_loop(1, PAIRS, send_k, 0)
     pltpu.make_async_copy(k_hbm.at[:, key_cols(z)], own.at[z, 0], sem_own.at[z]).start()
+    lax.fori_loop(1, PAIRS, send_v, 0)
+    vt[z] = v_ref[:, key_cols(z)].T
     pltpu.make_async_copy(vt.at[z], own.at[z, 1], sem_own.at[z]).start()
+
+    for n in range(NB):
+        lists[n, 0:2, 0:SPANS * SLOTS] = b_ref[:, n, :]
 
     def send_list(j, _):
         p = lax.rem(h + j, NB)
@@ -180,9 +194,10 @@
         wait(half(j, b + 2, 1), r4.at[j, 1])
         aside(j, b + 2)
 
-    def events(n):
-        for late, event in enumerate((event1, event2, event3, event4, event5)):
-            if 0 <= n - late < PAIRS:
+    def advance(n, kinds=(1, 2, 3, 4, 5)):
+        steps = zip(LAGS, (event1, event2, event3, event4, event5))
+        for kind, (late, event) in enumerate(steps, 1):
+            if kind in kinds and 0 <= n - late < PAIRS:
                 event(n - late)
 
     parity = (core, 1 - core)
@@ -257,16 +272,15 @@
         for i in range(2):
             qt[cc, i] = qbuf[cc, :, i * HD:(i + 1) * HD].T
 
-    for n in range(5):
-        events(n)
+    for n in range(-1, 5):
+        advance(n)
     wait(lst_v, sem_l.at[1])
     pltpu.make_async_copy(lst_v, lst, sem_l.at[3]).start()
     pltpu.make_async_copy(lst_v, lst, sem_l.at[3]).wait()
 
-    plan = {j: {1: 5 + j} for j in range(7)}
     for j in range(PAIRS):
         wait(kv[j][1], rs.at[j])
-        marks = plan.get(j, {})
+        advance(j + 5, (1, 2, 3, 4))
         if j == 0:
             def some(n, _):
                 pair = chip(n)
@@ -277,26 +291,22 @@
                 def _():
                     later_rows(0, pair)
 
-                for at, step in marks.items():
-                    @pl.when(n == at)
-                    def _():
-                        events(step)
+                @pl.when(n == 2)
+                def _():
+                    advance(j + 5, (5,))
                 return 0
 
             lax.fori_loop(0, PAIRS, some, 0)
             last_rows(0)
         else:
             last_rows(j)
-            if j + 1 < PAIRS:
-                def some(pair, _):
-                    later_rows(j, pair)
-                    for at, step in marks.items():
-                        @pl.when(pair == j + at)
-                        def _():
-                            events(step)
-                    return 0
-
-                lax.fori_loop(j + 1, PAIRS, some, 0)
+            advance(j + 5, (5,))
+
+            def some(pair, _):
+                later_rows(j, pair)
+                return 0
+
+            lax.fori_loop(j + 1, PAIRS, some, 0)
 
     wait(out_ref, sem_o.at[1])
 
@@ -320,16 +330,18 @@
 
 
 def body(queries, keys, values, blocks):
-    anywhere = pl.BlockSpec(memory_space=pl.ANY)
+    hbm = pl.BlockSpec(memory_space=pltpu.HBM)
     vmem = pl.BlockSpec(memory_space=pltpu.VMEM)
     dma = pltpu.SemaphoreType.DMA
     events = [dma((PAIRS, 2)) for _ in range(4)] + [dma((PAIRS,))]
     out = pl.pallas_call(
         kernel,
         out_shape=jax.ShapeDtypeStruct((BLOCK, queries.shape[2]), BF16),
-        in_specs=[anywhere, anywhere, vmem, vmem],
-        out_specs=vmem,
+        in_specs=[hbm] * 4,
+        out_specs=hbm,
         scratch_shapes=[pltpu.VMEM((NB, 2, BLOCK, HD), BF16) for _ in range(2 * PAIRS)] + [
+            pltpu.VMEM((BLOCK, PAIRS * HD), BF16),
+            pltpu.VMEM((2, NB, SPANS * SLOTS), jnp.int32),
             pltpu.VMEM((PAIRS, HD, BLOCK), BF16),
             pltpu.VMEM((PAIRS, 2, BLOCK, HD), BF16),
             pltpu.VMEM((SPANS, BLOCK, 2 * HD), BF16),
@@ -348,6 +360,7 @@
             dma((2,)),
             dma((4,)),
             dma((PAIRS,)),
+            dma((2,)),
         ] + events + events,
         compiler_params=pltpu.CompilerParams(
             collective_id=0, has_side_effects=True, vmem_limit_bytes=60 * 2**20),

time: 106 us -> 103 us (0.972)
  Pallas kernels: 104 us -> 100 us
    pallas_call x1, Pallas kernels: 104 us -> 100 us  [body(): pl.pallas_call(kernel, out_shape=jax.ShapeDtypeStruct((BLOCK, queries.sha...]
where the time goes in v4:
time: 103 us
  Pallas kernels  100 us (97%)
  local copies, waits for them, and re-layouts  2.29 us (2%)
    pallas_call x1, Pallas kernels, body(): pl.pallas_call(kernel, out_shape=jax.ShapeDtypeStruct((BLOCK, queries.sha...  100 us
    unnamed x1, local copies, waits for them, and re-layouts  2.29 us

profile of v4, /device:TPU:225, one launch (start us, length us, event | category | flops | bytes accessed | tf_op | source)
XLA Modules:
  0.0 102.8 jit_solution(3686369505063336172)
XLA Ops:
  0.0 100.5 %attend.1 = bf16[128,4096]{1,0:T(8,128)(2,1)} custom-call(bf16[128,4096]{1,0:T(8,128)(2,1)} %bitcast.6, bf16[128,1024]{1,0:T(8,128)(2,1)} %bitcast.7, bf16[128,1024]{1,0:T(8,128)(2,1)} %bitcast.8, s32[2,16,48]{2,1,0:T(8,128)} %bitcast.9), custom_call_target="tpu_custom_call" | custom-call | tf_op jit(solution)/shard_map/attend/pallas_call | solution.py:337
  100.5 2.3 %copy.6 = bf16[1,128,4096]{2,1,0:T(8,128)(2,1)} copy(bf16[1,128,4096]{2,1,0:T(8,128)(2,1)} %bitcast.5) | data formatting | bytes 2097152

commit v5 on v4

--- a/solution.py
+++ b/solution.py
@@ -256,8 +256,6 @@
                 parts = tiles_of(j, cc, i) + [(scores, 0.0, kv[j][t][here, 1])]
                 _, total, out = absorb(cc, i, parts, j == 0)
                 obuf[cc, :, i * HD:(i + 1) * HD] = (out / total).T.astype(BF16)
-        for t in range(2):
-            cc = 2 * j + parity[t]
 
             @pl.when(cc != c)
             def _():

time: 103 us -> 105 us (1.019)
  Pallas kernels: 100 us -> 102 us
    pallas_call x1, Pallas kernels: 100 us -> 102 us  [body(): pl.pallas_call(kernel, out_shape=jax.ShapeDtypeStruct((BLOCK, queries.sha...]
where the time goes in v5:
time: 105 us
  Pallas kernels  102 us (97%)
  local copies, waits for them, and re-layouts  2.29 us (2%)
    pallas_call x1, Pallas kernels, body(): pl.pallas_call(kernel, out_shape=jax.ShapeDtypeStruct((BLOCK, queries.sha...  102 us
    unnamed x1, local copies, waits for them, and re-layouts  2.29 us

profile of v5, /device:TPU:225, one launch (start us, length us, event | category | flops | bytes accessed | tf_op | source)
XLA Modules:
  0.0 104.8 jit_solution(12485581827331877519)
XLA Ops:
  0.0 102.5 %attend.1 = bf16[128,4096]{1,0:T(8,128)(2,1)} custom-call(bf16[128,4096]{1,0:T(8,128)(2,1)} %bitcast.6, bf16[128,1024]{1,0:T(8,128)(2,1)} %bitcast.7, bf16[128,1024]{1,0:T(8,128)(2,1)} %bitcast.8, s32[2,16,48]{2,1,0:T(8,128)} %bitcast.9), custom_call_target="tpu_custom_call" | custom-call | tf_op jit(solution)/shard_map/attend/pallas_call | solution.py:335
  102.5 2.3 %copy.6 = bf16[1,128,4096]{2,1,0:T(8,128)(2,1)} copy(bf16[1,128,4096]{2,1,0:T(8,128)(2,1)} %bitcast.5) | data formatting | bytes 2097152
